TPU v7x, 128 devices: a whole 4x4x4 slice. The times are simulated.
128 devices in a mesh: row: 8 (over z, core), col: 16 (over x, y).
Axes of the slice: x: 4, y: 4, z: 4, core: 2. Of those that a mesh axis runs over, the one named last changes fastest.
Arguments:
- front_block: bfloat16 [24576, 16384], P('row', 'col'), may hold values from -6 to 246, as said below
- child_blocks: bfloat16 [2, 16384, 8192], P(None, 'row', 'col'), may hold values from -6 to 6
- row_offsets: int32 [2, 16384], replicated, may hold values from -1 to 127, as said below
- tile_targets: int32 [2, 128], replicated, may hold values from 0 to 191, as said below
Outputs:
- factored: float32 [24576, 16384], P('row', 'col')
Inputs may be any that keep to these rules, and one draw needn't show every extreme that they name: `front_block`: entries on the front's natural diagonal lie between 114 and 246, the others between -6 and 6. `row_offsets`: within each tile of 128 child indices the entries that are not -1 are distinct and come first; each tile holds 64 or more of them. `tile_targets`: A child's tiles go to distinct front tiles; tile t goes to a front tile below 128 exactly when t < 64. Among one child's tiles with equal t % 8, exactly 2 go to front tiles of each value of tile % 8. Among the tiles t < 64 of both children with equal t % 16, at most 1 go to front tiles of one value of tile % 16, and 1 do for some value. Every value of tile % 16 receives the same number of a child's tiles t < 64, and every value of tile % 8 the same number of a child's tiles.
All inputs are finite; a program needn't handle non-finite values.
Results may differ from a plain program's by a relative error of at most 0.0017.
Values may be sent and summed in bfloat16 or wider, within the bound.
A program may use at most 192 MiB of HBM per device.

v0:
```python
import jax
import jax.numpy as jnp
from jax import lax
from jax.sharding import PartitionSpec as P

TILE = 128
PANEL = 256
PANELS = 2


def spread(value, axis, source):
    kept = jnp.where(lax.axis_index(axis) == source, value, 0).astype(value.dtype)
    return lax.psum(kept, axis)


def owner_ranks(owners):
    length = owners.shape[-1]
    same = owners[..., :, None] == owners[..., None, :]
    earlier = jnp.arange(length)[None, :] < jnp.arange(length)[:, None]
    return jnp.sum(same & earlier, axis=-1)


def row_table(tile_targets, row_count, local_tiles, cap_rows):
    owners = (tile_targets.reshape(2, local_tiles, row_count) % row_count).transpose(0, 2, 1)
    ranking = owner_ranks(owners)
    hits = (owners[:, :, None, None, :] == jnp.arange(row_count)[None, None, :, None, None]) & (
        ranking[:, :, None, None, :] == jnp.arange(cap_rows)[None, None, None, :, None]
    )
    return jnp.sum(jnp.where(hits, jnp.arange(local_tiles), 0), axis=-1)


def col_table(tile_targets, col_count, local_cols, cap_cols):
    heads = tile_targets[:, : local_cols * col_count].reshape(2, local_cols, col_count) % col_count
    owners = heads.reshape(2 * local_cols, col_count).T
    ranking = owner_ranks(owners)
    hits = (owners[:, None, None, :] == jnp.arange(col_count)[None, :, None, None]) & (
        ranking[:, None, None, :] == jnp.arange(cap_cols)[None, None, :, None]
    )
    chosen = jnp.sum(jnp.where(hits, jnp.arange(2 * local_cols), 0), axis=-1)
    return (chosen, jnp.any(hits, axis=-1))


def target_tiles(
    tile_targets,
    child_index,
    column_index,
    row_index,
    source_rows,
    source_cols,
    usable,
    row_count,
    col_count,
    row_tiles,
    shape,
):
    child_tile = row_index * row_count + source_rows
    col_tile = column_index * col_count + source_cols
    front_rows = tile_targets[child_index, child_tile] // row_count
    front_cols = tile_targets[child_index, col_tile] // col_count
    front_rows = jnp.where(usable, front_rows, row_tiles)
    return (front_rows.reshape(-1), jnp.broadcast_to(front_cols, shape).reshape(-1))


def share_column(column_piece, root):
    return spread(column_piece.astype(jnp.bfloat16), "col", root).astype(column_piece.dtype)


def share_pivot(pivot_piece, root):
    return spread(pivot_piece.astype(jnp.bfloat16), "row", root).astype(pivot_piece.dtype)


def update_block(working, factor_rows, factor_cols, live_rows, live_cols, begin_col, end_col):
    product = jnp.dot(
        factor_rows,
        factor_cols.T,
        precision=lax.Precision.HIGHEST,
        preferred_element_type=jnp.float32,
    )
    allowed = live_rows[:, None] & live_cols[None, begin_col:end_col]
    return working.at[:, begin_col:end_col].add(-jnp.where(allowed, product, 0.0))


def shards(front_block, child_blocks, row_offsets, tile_targets):
    R = lax.axis_size("row")
    Q = lax.axis_size("col")
    p = lax.axis_index("row")
    q = lax.axis_index("col")
    rows_local, cols_local = front_block.shape
    row_tiles = rows_local // TILE
    col_tiles = cols_local // TILE
    local_tiles = child_blocks.shape[1] // TILE
    local_cols = child_blocks.shape[2] // TILE
    cap_rows = local_tiles // R
    cap_cols = max(1, 2 * local_cols // Q)
    slot_ids = jnp.arange(TILE)
    own_offsets = row_offsets.reshape(2, local_tiles, R, TILE)[:, :, p]
    own_col_offsets = row_offsets[:, : local_cols * Q * TILE].reshape(2, local_cols, Q, TILE)[
        :, :, q
    ]
    row_hot = (own_offsets[:, :, None, :] == slot_ids[None, None, :, None]).astype(jnp.bfloat16)
    col_hot = (own_col_offsets[:, :, None, :] == slot_ids[None, None, :, None]).astype(jnp.bfloat16)
    blocks = child_blocks.reshape(2, local_tiles, TILE, local_cols, TILE)
    shifted = jnp.einsum(
        "cloi,clikj->clokj", row_hot, blocks, preferred_element_type=jnp.float32
    ).astype(jnp.bfloat16)
    placed = jnp.einsum(
        "clokj,ckzj->clokz", shifted, col_hot, preferred_element_type=jnp.float32
    ).astype(jnp.bfloat16)
    row_pick = row_table(tile_targets, R, local_tiles, cap_rows)
    col_pick, col_live = col_table(tile_targets, Q, local_cols, cap_cols)
    child_of = col_pick // local_cols
    within = col_pick % local_cols
    send_child = child_of[q]
    send_cols = within[q]
    send_live = col_live[q]
    recv_child = child_of[:, q]
    recv_cols = within[:, q]
    recv_live = col_live[:, q]
    own_rows = row_pick[:, p]
    their_rows = row_pick[:, :, p]
    child_send = send_child[None, :, :, None]
    row_index = own_rows[
        child_send, jnp.arange(R)[:, None, None, None], jnp.arange(cap_rows)[None, None, None, :]
    ]
    child_full = jnp.broadcast_to(child_send, row_index.shape)
    column_full = jnp.broadcast_to(send_cols[None, :, :, None], row_index.shape)
    picked = placed[child_full, row_index, :, column_full, :]
    picked = jnp.where(send_live[None, :, :, None, None, None], picked, jnp.zeros_like(picked))
    arrived = lax.all_to_all(
        picked.reshape(R * Q, cap_cols, cap_rows, TILE, TILE),
        ("row", "col"),
        split_axis=0,
        concat_axis=0,
        tiled=True,
    )
    child_recv = recv_child[None, :, :, None]
    column_recv = recv_cols[None, :, :, None]
    source_rows = jnp.arange(R)[:, None, None, None]
    source_cols = jnp.arange(Q)[None, :, None, None]
    row_recv = their_rows[child_recv, source_rows, jnp.arange(cap_rows)[None, None, None, :]]
    usable = recv_live[None, :, :, None]
    item_count = arrived.size // (TILE * TILE)
    index_shape = (item_count,)
    front_rows, front_cols = target_tiles(
        tile_targets,
        child_recv,
        column_recv,
        row_recv,
        source_rows,
        source_cols,
        usable,
        R,
        Q,
        row_tiles,
        row_recv.shape,
    )
    arrived_tiles = arrived.reshape(index_shape + (TILE, TILE)).astype(jnp.float32)
    summed = front_block.astype(jnp.float32).reshape(row_tiles, TILE, col_tiles, TILE)
    summed = summed.at[front_rows, :, front_cols, :].add(arrived_tiles, mode="drop")
    working = summed.reshape(rows_local, cols_local)
    row_spots = jnp.arange(rows_local)
    col_spots = jnp.arange(cols_local)
    nat_row = (row_spots // TILE * R + p) * TILE + row_spots % TILE
    nat_col = (col_spots // TILE * Q + q) * TILE + col_spots % TILE
    leading = None
    for section in range(PANELS):
        begin_col = section * PANEL
        finish = begin_col + PANEL
        panel_tiles = range(begin_col // TILE, finish // TILE)
        columns = []
        for f in panel_tiles:
            local_tile = f // Q
            source = working[:, local_tile * TILE : (local_tile + 1) * TILE]
            columns.append(share_column(source, f % Q))
        panel_block = jnp.concatenate(columns, axis=1)
        pivots = []
        for f in panel_tiles:
            local_tile = f // R
            pivots.append(
                share_pivot(panel_block[local_tile * TILE : (local_tile + 1) * TILE], f % R)
            )
        pivot_block = jnp.linalg.cholesky(jnp.concatenate(pivots, axis=0))
        solved = lax.linalg.triangular_solve(
            pivot_block, panel_block, left_side=False, lower=True, transpose_a=True
        )
        relative = nat_row - begin_col
        inside = pivot_block[jnp.clip(relative, 0, PANEL - 1)]
        factor_rows = jnp.where(
            relative[:, None] >= PANEL, solved, jnp.where(relative[:, None] >= 0, inside, 0.0)
        )
        pick_tiles = jnp.arange(col_tiles) * (Q // R) + q // R
        chosen = factor_rows.reshape(row_tiles, TILE, PANEL)[pick_tiles].reshape(cols_local, PANEL)
        factor_cols = spread(chosen.astype(jnp.bfloat16), "row", q % R).astype(chosen.dtype)
        live_rows = nat_row >= finish
        live_cols = nat_col >= finish
        working = update_block(
            working, factor_rows, factor_cols, live_rows, live_cols, 0, cols_local
        )
        for f in panel_tiles:
            local_tile = f // Q
            offset_col = (f - begin_col // TILE) * TILE
            fresh = factor_rows[:, offset_col : offset_col + TILE]
            former = working[:, local_tile * TILE : (local_tile + 1) * TILE]
            working = working.at[:, local_tile * TILE : (local_tile + 1) * TILE].set(
                jnp.where(q == f % Q, fresh, former)
            )
    return working


def solution(mesh):
    return jax.shard_map(
        shards,
        mesh=mesh,
        in_specs=(P("row", "col"), P(None, "row", "col"), P(), P()),
        out_specs=P("row", "col"),
        check_vma=False,
    )
```

profile of v0, /device:TPU:0, one launch (start us, length us, event | category | flops | bytes accessed | tf_op | source)
XLA Modules:
  0.0 955.4 jit_solution(5208802484082375721)
XLA Ops:
  10.4 2.8 gather_fusion.3
  13.9 6.9 reshape.983
  20.9 6.5 convert_bitcast_fusion.1
  27.4 13.0 %gather_fusion.4 = bf16[256,128,128]{1,2,0:T(8,128)(2,1)} fusion(bf16[2,16,128,4,128]{2,4,1,3,0:T(8,128)(2,1)} %convert_bitcast_fusion.1, s32[256]{0:T(256)S(1)} %reshape.1048), kind=kCustom, calls=%fused_computation.4 | custom fusion | bytes 16780288 | tf_op jit(solution)/shard_map/gather | solution.py:127
  40.5 7.2 broadcast_select_fusion
  47.7 11.7 %all-to-all-start = ((bf16[128,1,2,128,128]{3,4,2,1,0:T(8,128)(2,1)}), bf16[128,1,2,128,128]{3,4,2,1,0:T(8,128)(2,1)}, u32[]{:S(2)}, u32[]{:S(2)}) async-start(bf16[128,1,2,128,128]{3,4,2,1,0:T(8,128)(2,1)} %broadcast_select_fusion), calls=%async_computation | async-start | bytes 16777216 | tf_op jit(solution)/shard_map/all_to_all | solution.py:129
  60.1 2.8 gather_fusion
  63.5 2.4 gather_fusion.1
  67.5 9.1 convert_bitcast_fusion
  76.7 12.3 %copy.105 = f32[384,8,8,128]{3,2,1,0:T(8,128)} copy(f32[384,8,8,128]{3,1,2,0:T(8,128)} %convert_bitcast_fusion) | data formatting | bytes 25165824
  88.9 11.7 %copy.83 = f32[24,128,8,128]{3,1,2,0:T(8,128)} copy(f32[24,128,8,128]{3,2,1,0:T(8,128)} %bitcast.209) | data formatting | bytes 25165824 | tf_op jit(solution)/shard_map/reshape | solution.py:158
  100.6 57.9 %all-to-all-done = bf16[128,1,2,128,128]{3,4,2,1,0:T(8,128)(2,1)} async-done(((bf16[128,1,2,128,128]{3,4,2,1,0:T(8,128)(2,1)}), bf16[128,1,2,128,128]{3,4,2,1,0:T(8,128)(2,1)}, u32[]{:S(2)}, u32[]{:S(2)}) %all-to-all-start) | async-done | bytes 8388640 | tf_op jit(solution)/shard_map/all_to_all | solution.py:129
  158.5 11.2 %bitcast_convert_fusion = f32[256,128,128]{1,2,0:T(8,128)} fusion(bf16[128,1,2,128,128]{3,4,2,1,0:T(8,128)(2,1)} %all-to-all-done), kind=kLoop, calls=%fused_computation.18 | loop fusion | flops 4194304 | bytes 25165824 | tf_op jit(solution)/shard_map/convert_element_type | solution.py:157
  169.8 17.4 %copy.84 = f32[256,128,128]{2,1,0:T(8,128)} copy(f32[256,128,128]{1,2,0:T(8,128)} %bitcast_convert_fusion) | data formatting | bytes 33554432 | tf_op jit(solution)/shard_map/convert_element_type | solution.py:157
  187.2 53.8 %scatter_fusion = f32[24,128,8,128]{3,1,2,0:T(8,128)} fusion(f32[24,128,8,128]{3,1,2,0:T(8,128)} %copy.83, s32[256]{0:T(256)S(1)} %bitcast.211, f32[256,128,128]{2,1,0:T(8,128)} %copy.84), kind=kCustom, calls=%fused_computation.9 | custom fusion | flops 4194304 | bytes 50333696 | tf_op jit(solution)/shard_map/scatter-add | solution.py:159
  241.0 13.0 %copy.85 = f32[24,128,8,128]{1,0,3,2:T(8,128)} copy(f32[24,128,8,128]{3,1,2,0:T(8,128)} %scatter_fusion) | data formatting | bytes 25165824 | tf_op jit(solution)/shard_map/scatter-add | solution.py:159
  254.0 7.7 copy.119
  265.0 89.9 %all-reduce.18.cloned.1.call-done = (bf16[3072,128]{0,1:T(8,128)(2,1)}, bf16[3072,128]{0,1:T(8,128)(2,1)}) async-done(((bf16[3072,128]{0,1:T(8,128)(2,1)}, bf16[3072,128]{0,1:T(8,128)(2,1)}), (bf16[3072,128]{0,1:T(8,128)(2,1)}, bf16[3072,128]{0,1:T(8,128)(2,1)})) %all-reduce.18.cloned.1.call-update) | async-done | bytes 1572880 | tf_op jit(solution)/shard_map/psum | solution.py:13
  361.5 56.7 %all-reduce.22.cloned.1.call-done = (bf16[128,256]{0,1:T(8,128)(2,1)}, bf16[128,256]{0,1:T(8,128)(2,1)}) async-done(((bf16[128,256]{0,1:T(8,128)(2,1)}, bf16[128,256]{0,1:T(8,128)(2,1)}), (bf16[128,256]{0,1:T(8,128)(2,1)}, bf16[128,256]{0,1:T(8,128)(2,1)})) %all-reduce.22.cloned.1.call-update) | async-done | bytes 131088 | tf_op jit(solution)/shard_map/psum | solution.py:13
  422.5 11.7 %cholesky.130 = f32[128,128]{1,0:T(8,128)S(1)} custom-call(f32[128,128]{1,0:T(8,128)S(1)} %cholesky.194), custom_call_target="Cholesky" | custom-call | tf_op jit(solution)/shard_map/jit(cholesky)/cholesky | solution.py:182
  434.8 9.8 %custom-call.25 = f32[1,128,128]{1,2,0:T(8,128)S(1)} custom-call(f32[1,128,128]{2,1,0:T(8,128)S(1)} %get-tuple-element.163), custom_call_target="InvertDiagBlocksLowerTriangular" | custom-call | tf_op jit(solution)/shard_map/jit(cholesky)/cholesky | solution.py:182
  446.8 11.7 %cholesky.147 = f32[128,128]{1,0:T(8,128)S(1)} custom-call(f32[128,128]{1,0:T(8,128)S(1)} %convolution_subtract_fusion.3), custom_call_target="Cholesky" | custom-call | tf_op jit(solution)/shard_map/jit(cholesky)/cholesky | solution.py:182
  463.6 12.5 %gather_fusion.5 = f32[3072,256]{1,0:T(8,128)} fusion(f32[256,256]{1,0:T(8,128)S(1)} %get-tuple-element.141, s32[3072]{0:T(1024)S(1)} %broadcast_clamp_fusion.1), kind=kCustom, calls=%fused_computation.5 | custom fusion | bytes 6303744 | tf_op jit(solution)/shard_map/gather | solution.py:187
  476.1 3.6 copy.88
  479.8 4.1 while.12
  484.6 20.5 %custom-call.26 = f32[2,128,128]{1,2,0:T(8,128)S(1)} custom-call(f32[2,128,128]{2,1,0:T(8,128)} %copy-done.17), custom_call_target="InvertDiagBlocksLowerTriangular" | custom-call | tf_op jit(solution)/shard_map/triangular_solve/custom-call.0 | solution.py:183
  512.4 2.9 gather_fusion.6
  517.9 58.8 %all-reduce.12.cloned.1.call-done = bf16[1024,256]{1,0:T(8,128)(2,1)} async-done(((bf16[1024,256]{1,0:T(8,128)(2,1)}), bf16[1024,256]{1,0:T(8,128)(2,1)}) %all-reduce.12.cloned.1.call-update) | async-done | bytes 524304 | tf_op jit(solution)/shard_map/psum | solution.py:13
  576.7 11.8 %negate_add_fusion.1 = f32[3072,1024]{0,1:T(8,128)S(1)} fusion(f32[3072,256]{0,1:T(8,128)S(1)} %maximum_select_fusion, bf16[1024,256]{1,0:T(8,128)(2,1)} %all-reduce.12.cloned.1.call-done, pred[3072]{0:T(1024)(128)(4,1)S(1)} %get-tuple-element.181, pred[1024]{0:T(1024)(128)(4,1)S(1)} %broadcast_compare_fusion.4, f32[128,8,24,128]{3,2,1,0:T(8,128)} %bitcast.208), kind=kOutput, calls=%fused_computation.17 | convolution fusion | flops 9676259328 | bytes 28839936 | tf_op jit(solution)/shard_map/dot_general | solution.py:73
  588.5 4.8 copy-done.1
  593.3 2.5 broadcast_select_fusion.1
  598.0 86.6 %all-reduce.16.cloned.1.call-done = (bf16[3072,128]{0,1:T(8,128)(2,1)}, bf16[3072,128]{0,1:T(8,128)(2,1)}) async-done(((bf16[3072,128]{0,1:T(8,128)(2,1)}, bf16[3072,128]{0,1:T(8,128)(2,1)}), (bf16[3072,128]{0,1:T(8,128)(2,1)}, bf16[3072,128]{0,1:T(8,128)(2,1)})) %all-reduce.16.cloned.1.call-update) | async-done | bytes 1572880 | tf_op jit(solution)/shard_map/psum | solution.py:13
  691.5 56.5 %all-reduce.20.cloned.1.call-done = (bf16[128,256]{0,1:T(8,128)(2,1)}, bf16[128,256]{0,1:T(8,128)(2,1)}) async-done(((bf16[128,256]{0,1:T(8,128)(2,1)}, bf16[128,256]{0,1:T(8,128)(2,1)}), (bf16[128,256]{0,1:T(8,128)(2,1)}, bf16[128,256]{0,1:T(8,128)(2,1)})) %all-reduce.20.cloned.1.call-update) | async-done | bytes 131088 | tf_op jit(solution)/shard_map/psum | solution.py:13
  752.3 11.7 %cholesky.164 = f32[128,128]{1,0:T(8,128)S(1)} custom-call(f32[128,128]{1,0:T(8,128)S(1)} %cholesky.197), custom_call_target="Cholesky" | custom-call | tf_op jit(solution)/shard_map/jit(cholesky)/cholesky | solution.py:182
  764.6 9.8 %custom-call.27 = f32[1,128,128]{1,2,0:T(8,128)S(1)} custom-call(f32[1,128,128]{2,1,0:T(8,128)S(1)} %get-tuple-element.159), custom_call_target="InvertDiagBlocksLowerTriangular" | custom-call | tf_op jit(solution)/shard_map/jit(cholesky)/cholesky | solution.py:182
  776.6 11.7 %cholesky.181 = f32[128,128]{1,0:T(8,128)S(1)} custom-call(f32[128,128]{1,0:T(8,128)S(1)} %convolution_subtract_fusion.2), custom_call_target="Cholesky" | custom-call | tf_op jit(solution)/shard_map/jit(cholesky)/cholesky | solution.py:182
  793.1 12.7 %gather_fusion.7 = f32[3072,256]{1,0:T(8,128)} fusion(f32[256,256]{1,0:T(8,128)S(1)} %get-tuple-element.136, s32[3072]{0:T(1024)S(1)} %broadcast_clamp_fusion), kind=kCustom, calls=%fused_computation.7 | custom fusion | bytes 6303744 | tf_op jit(solution)/shard_map/gather | solution.py:187
  805.8 3.6 copy.93
  809.5 3.7 while.13
  813.8 20.5 %custom-call.28 = f32[2,128,128]{1,2,0:T(8,128)S(1)} custom-call(f32[2,128,128]{2,1,0:T(8,128)} %copy-done.16), custom_call_target="InvertDiagBlocksLowerTriangular" | custom-call | tf_op jit(solution)/shard_map/triangular_solve/custom-call.0 | solution.py:183
  841.2 2.9 gather_fusion.8
  846.0 3.9 fusion.23
  849.8 55.6 %all-reduce.14.cloned.1.call-done = bf16[1024,256]{1,0:T(8,128)(2,1)} async-done(((bf16[1024,256]{1,0:T(8,128)(2,1)}), bf16[1024,256]{1,0:T(8,128)(2,1)}) %all-reduce.14.cloned.1.call-update) | async-done | bytes 524304 | tf_op jit(solution)/shard_map/psum | solution.py:13
  905.5 12.7 %negate_add_fusion = f32[3072,1024]{0,1:T(8,128)} fusion(f32[3072,1024]{0,1:T(8,128)} %fusion.23, f32[3072,256]{0,1:T(8,128)S(1)} %maximum_select_fusion.1, bf16[1024,256]{1,0:T(8,128)(2,1)} %all-reduce.14.cloned.1.call-done, pred[3072]{0:T(1024)(128)(4,1)S(1)} %broadcast_compare_fusion, pred[1024]{0:T(1024)(128)(4,1)S(1)} %copy-done.22), kind=kOutput, calls=%fused_computation.16 | convolution fusion | flops 9676259328 | bytes 28839936 | tf_op jit(solution)/shard_map/dot_general | solution.py:73
  918.1 10.7 %copy.154 = f32[3072,1024]{0,1:T(8,128)} copy(f32[3072,1024]{0,1:T(8,128)} %negate_add_fusion) | data formatting | bytes 25165824
  928.9 3.4 fusion.24
  932.2 3.5 fusion.13
  935.7 12.6 %copy.96 = f32[3072,1024]{1,0:T(8,128)} copy(f32[3072,1024]{0,1:T(8,128)} %fusion.13) | data formatting | bytes 25165824 | tf_op jit(solution)/shard_map/scatter | solution.py:204
  (211 shorter events, 75.2 us)
Async XLA Ops:
  10.4 3.4 copy-start.15
  47.7 110.8 %all-to-all-start = ((bf16[128,1,2,128,128]{3,4,2,1,0:T(8,128)(2,1)}), bf16[128,1,2,128,128]{3,4,2,1,0:T(8,128)(2,1)}, u32[]{:S(2)}, u32[]{:S(2)}) async-start(bf16[128,1,2,128,128]{3,4,2,1,0:T(8,128)(2,1)} %broadcast_select_fusion), calls=%async_computation | async-start | bytes 16777216 | tf_op jit(solution)/shard_map/all_to_all | solution.py:129
  59.4 295.5 %all-reduce.18.cloned.1.call-start = ((), (), s32[]{:S(2)}) async-start(), calls=%async_computation.4 | async-start | bytes 3145728 | tf_op jit(solution)/shard_map/psum | solution.py:13
  62.9 0.7 copy-start
  263.0 155.2 %all-reduce.22.cloned.1.call-start = ((), (), s32[]{:S(2)}) async-start(), calls=%async_computation.6 | async-start | bytes 262144 | tf_op jit(solution)/shard_map/psum | solution.py:13
  357.3 1.1 copy-start.6
  359.1 217.6 %all-reduce.12.cloned.1.call-start = ((), (), s32[]{:S(2)}) async-start(), calls=%async_computation.1 | async-start | bytes 1048576 | tf_op jit(solution)/shard_map/psum | solution.py:13
  421.8 0.7 copy-start.13
  458.5 3.3 copy-start.11
  476.1 3.6 copy-start.25
  476.1 3.7 copy-start.10
  483.9 0.7 copy-start.17
  484.6 20.5 %copy-start.23 = (s32[2,2]{1,0:T(2,128)}, s32[2,2]{1,0:T(2,128)S(1)}, u32[]{:S(2)}) copy-start(s32[2,2]{1,0:T(2,128)S(1)} %get-tuple-element.323) | copy-start | bytes 52
  506.6 3.2 copy-start.5
  506.6 3.2 copy-start.21
  510.2 78.3 %copy-start.2 = (f32[3072,256]{0,1:T(8,128)}, f32[3072,256]{0,1:T(8,128)S(1)}, u32[]{:S(2)}) copy-start(f32[3072,256]{0,1:T(8,128)S(1)} %maximum_select_fusion) | copy-start | bytes 9437188
  517.2 167.4 %all-reduce.16.cloned.1.call-start = ((), (), s32[]{:S(2)}) async-start(), calls=%async_computation.3 | async-start | bytes 3145728 | tf_op jit(solution)/shard_map/psum | solution.py:13
  588.5 4.8 copy-start.1
  595.8 2.2 copy-start.18
  595.8 93.4 %copy-start.3 = (f32[3072,128]{0,1:T(8,128)S(1)}, f32[3072,128]{0,1:T(8,128)}, u32[]{:S(2)}) copy-start(f32[3072,128]{0,1:T(8,128)} %get-tuple-element.139) | copy-start | bytes 4718596
  596.8 151.3 %all-reduce.20.cloned.1.call-start = ((), (), s32[]{:S(2)}) async-start(), calls=%async_computation.5 | async-start | bytes 262144 | tf_op jit(solution)/shard_map/psum | solution.py:13
  687.0 1.2 copy-start.7
  688.9 216.5 %all-reduce.14.cloned.1.call-start = ((), (), s32[]{:S(2)}) async-start(), calls=%async_computation.2 | async-start | bytes 1048576 | tf_op jit(solution)/shard_map/psum | solution.py:13
  689.2 2.0 copy-start.8
  751.6 0.7 copy-start.14
  788.3 3.1 copy-start.12
  805.8 3.6 copy-start.9
  805.8 3.6 copy-start.24
  813.1 0.6 copy-start.16
  835.8 3.2 copy-start.4
  835.8 3.2 copy-start.19
  835.8 3.2 copy-start.20
  844.1 61.4 %copy-start.22 = (pred[1024]{0:T(1024)(128)(4,1)S(1)}, pred[1024]{0:T(1024)(128)(4,1)}, u32[]{:S(2)}) copy-start(pred[1024]{0:T(1024)(128)(4,1)} %broadcast_compare_fusion.3) | copy-start | bytes 3076
Sparse Core Ops, SparseCore 0:
  263.1 91.7 all-reduce.17
  359.2 58.9 all-reduce.21
  517.3 59.3 all-reduce.11
  596.9 87.6 all-reduce.15
  689.0 58.9 all-reduce.19
  846.1 59.3 all-reduce.13
where the time goes:
time: 965 us; the launch traced here: 955 us
  waiting for transfers between devices  462 us (48%)
  other arithmetic  232 us (24%)
  local copies, waits for them, and re-layouts  187 us (19%)
  matrix products  44.5 us (5%)
  between operations  17.1 us (2%)
  starting transfers between devices  12.3 us (1%)
    psum x6, waiting for transfers between devices, spread(): return lax.psum(kept, axis)  404 us
    another operation x14, other arithmetic, shards(): pivot_block = jnp.linalg.cholesky(jnp.concatenate(pivots, axis=0))  71.5 us
    all_to_all x1, waiting for transfers between devices, shards(): lax.all_to_all(picked.reshape(R * Q, cap_cols, cap_rows, TILE, TILE), ('r...  57.9 us
    scatter-add x1, other arithmetic, shards(): summed.at[front_rows, :, front_cols, :].add(arrived_tiles, mode='drop')  53.8 us
    another operation x5, other arithmetic, shards(): lax.linalg.triangular_solve(pivot_block, panel_block, left_side=False, lo...  45 us
    unnamed x60, local copies, waits for them, and re-layouts  43.7 us
    gather x4, local copies, waits for them, and re-layouts, shards(): inside = pivot_block[jnp.clip(relative, 0, PANEL - 1)]  32.4 us
    dot_general x2, matrix products, update_block(): jnp.dot(factor_rows, factor_cols.T, precision=lax.Precision.HIGHEST, pref...  24.5 us
  transfers between devices with their start and end apart: 7, of which 7 were waited for; matrix products, arithmetic and copies ran while one was open for 5% of the time, Pallas kernels for 0%

commit v1 on v0

v1 whole, which is shorter than its diff:
```python
import jax
import jax.numpy as jnp
from jax import lax
from jax.experimental import pallas as pl
from jax.experimental.pallas import tpu as pltpu
from jax.sharding import PartitionSpec as P

TILE = 128
ROWS = 8
COLS = 16
DEVICES = ROWS * COLS
MESH = pl.DeviceIdType.MESH
VMEM_LIMIT = 56 * 2**20
BF16 = jnp.bfloat16
F32 = jnp.float32
NT = (((1,), (1,)), ((), ()))


def spec(space):
    return pl.BlockSpec(memory_space=space)


def iota(dim):
    return lax.broadcasted_iota(jnp.int32, (TILE, TILE), dim)


def one_hot(offsets):
    return jnp.where(iota(0) == offsets, 1.0, 0.0).astype(BF16)


def place_kernel(targets, where, offsets, child, front, picked, corner, shifted, rank, seen):
    p = where[0]
    q = where[1]
    corner[...] = jnp.zeros_like(corner)

    @pl.when((p < 4) & (q < 4))
    def _():
        corner[p * 4 + q] = front[...].astype(F32)

    for c in range(2):
        for d in range(ROWS):
            seen[d] = 0

        def order(l, carry):
            owner = lax.rem(targets[c, l * ROWS + p], ROWS)
            rank[l] = owner * COLS * 2 + seen[owner]
            seen[owner] = seen[owner] + 1
            return carry

        lax.fori_loop(0, 16, order, 0)

        def shift(l, carry):
            hot = one_hot(offsets[c, pl.ds(l * ROWS + p, 1), :])
            at = pl.ds(pl.multiple_of(l * TILE, TILE), TILE)
            moved = jnp.dot(hot, child[c, at, :], preferred_element_type=F32)
            shifted[at, :] = moved.astype(BF16)
            return carry

        lax.fori_loop(0, 16, shift, 0, unroll=4)
        for k in range(4):
            hot = one_hot(offsets[c, pl.ds(k * COLS + q, 1), :])
            front_col = targets[c, k * COLS + q]
            base = lax.rem(front_col, COLS) * 2
            for part in range(4):
                rows = shifted[part * 512 : (part + 1) * 512, k * TILE : (k + 1) * TILE]
                placed = lax.dot_general(rows, hot, NT, preferred_element_type=F32)
                for s in range(4):
                    l = part * 4 + s
                    tile = placed[s * TILE : (s + 1) * TILE]
                    picked[rank[l] + base] = tile.astype(BF16)
                    front_row = targets[c, l * ROWS + p]

                    @pl.when((front_row < 4) & (front_col < 4))
                    def _(tile=tile, front_row=front_row, front_col=front_col):
                        corner[front_row * 4 + front_col] += tile


def place(targets, where, offsets, child, front):
    return pl.pallas_call(
        place_kernel,
        out_shape=(
            jax.ShapeDtypeStruct((DEVICES * 2, TILE, TILE), BF16),
            jax.ShapeDtypeStruct((16, TILE, TILE), F32),
        ),
        in_specs=[spec(pltpu.SMEM), spec(pltpu.SMEM)] + [spec(pltpu.VMEM)] * 3,
        out_specs=(spec(pltpu.VMEM), spec(pltpu.VMEM)),
        scratch_shapes=[
            pltpu.VMEM((16 * TILE, 4 * TILE), BF16),
            pltpu.SMEM((16,), jnp.int32),
            pltpu.SMEM((ROWS,), jnp.int32),
        ],
        compiler_params=pltpu.CompilerParams(vmem_limit_bytes=VMEM_LIMIT),
        cost_estimate=pl.CostEstimate(flops=2**31, bytes_accessed=14 * 2**20, transcendentals=0),
        name="place",
    )(targets, where, offsets, child, front)


def corner_kernel(part, whole, held, send, recv, send_sum, recv_sum, local):
    p = lax.axis_index("row")
    q = lax.axis_index("col")
    me = p * COLS + q
    barrier = pltpu.get_barrier_semaphore()

    def greet(d, carry):
        t = lax.rem(me + d, DEVICES)
        pl.semaphore_signal(
            barrier, inc=1, device_id=(t // COLS, lax.rem(t, COLS)), device_id_type=MESH
        )
        return carry

    lax.fori_loop(1, DEVICES, greet, 0)
    pl.semaphore_wait(barrier, DEVICES - 1)
    own = pltpu.make_async_copy(part.at[me], held.at[me], local)
    own.start()

    def scatter(d, carry):
        t = lax.rem(me + d, DEVICES)
        pltpu.make_async_remote_copy(
            part.at[t],
            held.at[me],
            send,
            recv,
            device_id=(t // COLS, lax.rem(t, COLS)),
            device_id_type=MESH,
        ).start()
        return carry

    lax.fori_loop(1, DEVICES, scatter, 0)
    own.wait()
    others = pl.ds(0, DEVICES - 1)
    pltpu.make_async_copy(held.at[others], held.at[others], recv).wait()
    whole[me] = jnp.sum(held[...], axis=0)

    def gather(d, carry):
        t = lax.rem(me + d, DEVICES)
        pltpu.make_async_remote_copy(
            whole.at[me],
            whole.at[me],
            send_sum,
            recv_sum,
            device_id=(t // COLS, lax.rem(t, COLS)),
            device_id_type=MESH,
        ).start()
        return carry

    lax.fori_loop(1, DEVICES, gather, 0)
    pltpu.make_async_copy(part.at[others], part.at[others], send).wait()
    pltpu.make_async_copy(whole.at[others], whole.at[others], send_sum).wait()
    pltpu.make_async_copy(whole.at[others], whole.at[others], recv_sum).wait()


def sum_corner(part):
    return pl.pallas_call(
        corner_kernel,
        out_shape=jax.ShapeDtypeStruct((DEVICES, 16, TILE), F32),
        in_specs=[spec(pltpu.VMEM)],
        out_specs=spec(pltpu.VMEM),
        scratch_shapes=[pltpu.VMEM((DEVICES, 16, TILE), F32)] + [pltpu.SemaphoreType.DMA] * 5,
        compiler_params=pltpu.CompilerParams(
            collective_id=1, has_side_effects=True, vmem_limit_bytes=VMEM_LIMIT
        ),
        cost_estimate=pl.CostEstimate(flops=2**18, bytes_accessed=2**22, transcendentals=0),
        name="corner",
    )(part)


def mm(a, b):
    return jnp.dot(a, b, precision=lax.Precision.HIGHEST, preferred_element_type=F32)


def mm_nt(a, b):
    return lax.dot_general(
        a, b, NT, precision=lax.Precision.HIGHEST, preferred_element_type=F32
    )


def factor_tile(a):
    blocks = TILE // 8
    sub = lax.broadcasted_iota(jnp.int32, (8, 1), 0)
    eye = jnp.where(iota(0) == iota(1), 1.0, 0.0)
    upper = [a[i * 8 : (i + 1) * 8] for i in range(blocks)]
    inverse = [eye[i * 8 : (i + 1) * 8] for i in range(blocks)]
    for s in range(TILE):
        b, r = s // 8, s % 8
        u_row = upper[b][r : r + 1]
        i_row = inverse[b][r : r + 1]
        scale = 1.0 / u_row[:, s : s + 1]
        u_row = u_row * scale
        i_row = i_row * scale
        for i in range(b, blocks):
            column = upper[i][:, s : s + 1]
            if i == b:
                if r == 7:
                    continue
                column = jnp.where(sub > r, column, 0.0)
            upper[i] = upper[i] - column * u_row
            inverse[i] = inverse[i] - column * i_row
    u = jnp.concatenate(upper, axis=0)
    inv = jnp.concatenate(inverse, axis=0)
    diagonal = jnp.sum(jnp.where(iota(0) == iota(1), u, 0.0), axis=1, keepdims=True)
    root = lax.rsqrt(diagonal)
    u = jnp.where(iota(1) >= iota(0), u * root, 0.0)
    return u.T, inv * root


def factor_kernel(corner, lower, inverse, work, inv):
    def symmetric(i, j):
        return (corner[i * 4 + j] + corner[j * 4 + i].T) * 0.5

    for i in range(4):
        for j in range(i + 1):
            work[i * 4 + j] = symmetric(i, j) if i // 2 == j // 2 else corner[i * 4 + j]
    lower[...] = jnp.zeros_like(lower)

    def panel(j, carry):
        pivot, pivot_inv = factor_tile(work[j * 5])
        lower[j * 5] = pivot
        inv[j * 5] = pivot_inv

        def solve(i, carry):
            lower[i * 4 + j] = mm_nt(work[i * 4 + j], pivot_inv)
            return carry

        lax.fori_loop(j + 1, 4, solve, 0)

        def update_row(i, carry):
            def update(k, carry):
                work[i * 4 + k] -= mm_nt(lower[i * 4 + j], lower[k * 4 + j])
                return carry

            return lax.fori_loop(j + 1, i + 1, update, carry)

        lax.fori_loop(j + 1, 4, update_row, 0)
        return carry

    lax.fori_loop(0, 4, panel, 0)
    inverse[...] = jnp.zeros_like(inverse)
    for j in range(4):
        column = {j: inv[j * 5]}
        for i in range(j + 1, 4):
            total = mm(lower[i * 4 + j], column[j])
            for k in range(j + 1, i):
                total = total + mm(lower[i * 4 + k], column[k])
            column[i] = -mm(inv[i * 5], total)
        for i in range(j, 4):
            inverse[i * TILE : (i + 1) * TILE, j * TILE : (j + 1) * TILE] = column[i].astype(BF16)


def factor(corner):
    return pl.pallas_call(
        factor_kernel,
        out_shape=(
            jax.ShapeDtypeStruct((16, TILE, TILE), F32),
            jax.ShapeDtypeStruct((4 * TILE, 4 * TILE), BF16),
        ),
        in_specs=[spec(pltpu.VMEM)],
        out_specs=(spec(pltpu.VMEM), spec(pltpu.VMEM)),
        scratch_shapes=[pltpu.VMEM((16, TILE, TILE), F32), pltpu.VMEM((16, TILE, TILE), F32)],
        compiler_params=pltpu.CompilerParams(vmem_limit_bytes=VMEM_LIMIT),
        cost_estimate=pl.CostEstimate(flops=2**30, bytes_accessed=2**22, transcendentals=0),
        name="factor",
    )(corner)


def index_rows(targets, p, row_from, seen):
    def clear(i, carry):
        row_from[i] = -1
        return carry

    lax.fori_loop(0, 48, clear, 0)
    for c in range(2):
        for d in range(ROWS):
            seen[d] = 0

        def visit(t, carry):
            goal = targets[c, t]

            @pl.when(lax.rem(goal, ROWS) == p)
            def _():
                source = lax.rem(t, ROWS)
                row_from[c * 24 + goal // ROWS] = source * COLS * 2 + seen[source]
                seen[source] = seen[source] + 1

            return carry

        lax.fori_loop(0, 128, visit, 0)


def index_cols(targets, q, col_from):
    for i in range(16):
        col_from[i] = -1
    for c in range(2):

        def visit(t, carry):
            goal = targets[c, t]

            @pl.when(lax.rem(goal, COLS) == q)
            def _():
                col_from[c * 8 + goal // COLS] = lax.rem(t, COLS) * 2

            return carry

        lax.fori_loop(0, 64, visit, 0)


def column_kernel(targets, where, front, arrived, column, total, row_from, col_from, seen):
    p = where[0]
    q = where[1]

    @pl.when(q < 4)
    def _():
        index_rows(targets, p, row_from, seen)
        index_cols(targets, q, col_from)

        def tile(l, carry):
            total[...] = front[pl.ds(pl.multiple_of(l * TILE, TILE), TILE), :].astype(F32)
            for c in range(2):
                row, col = row_from[c * 24 + l], col_from[c * 8]

                @pl.when((row >= 0) & (col >= 0))
                def _(row=row, col=col):
                    total[...] += arrived[row + col].astype(F32)

            column[l] = total[...].astype(BF16)
            return carry

        lax.fori_loop(0, 24, tile, 0)


def first_column(targets, where, front, arrived):
    return pl.pallas_call(
        column_kernel,
        out_shape=jax.ShapeDtypeStruct((24, TILE, TILE), BF16),
        grid=(1,),
        in_specs=[
            spec(pltpu.SMEM),
            spec(pltpu.SMEM),
            pl.BlockSpec((24 * TILE, TILE), lambda i: (0, 0)),
            pl.BlockSpec((DEVICES * 2, TILE, TILE), lambda i: (0, 0, 0)),
        ],
        out_specs=pl.BlockSpec((24, TILE, TILE), lambda i: (0, 0, 0)),
        scratch_shapes=[
            pltpu.VMEM((TILE, TILE), F32),
            pltpu.SMEM((48,), jnp.int32),
            pltpu.SMEM((16,), jnp.int32),
            pltpu.SMEM((ROWS,), jnp.int32),
        ],
        compiler_params=pltpu.CompilerParams(vmem_limit_bytes=VMEM_LIMIT),
        cost_estimate=pl.CostEstimate(flops=2**20, bytes_accessed=2**23, transcendentals=0),
        name="column",
    )(targets, where, front, arrived)


def spread_kernel(column, rows, cols, sends, recvs, local):
    p = lax.axis_index("row")
    q = lax.axis_index("col")
    z, core = p // 2, lax.rem(p, 2)
    x, y = q // 4, lax.rem(q, 4)

    def at_x(d):
        return (p, lax.rem(x + d, 4) * 4 + y)

    def at_y(d):
        return (p, x * 4 + lax.rem(y + d, 4))

    def at_z(d):
        return (lax.rem(z + d, 4) * 2 + core, q)

    sibling = (z * 2 + 1 - core, q)
    barrier = pltpu.get_barrier_semaphore()
    for d in (1, 2, 3):
        for peer in (at_x(d), at_y(d), at_z(d)):
            pl.semaphore_signal(barrier, inc=1, device_id=peer, device_id_type=MESH)
    pl.semaphore_signal(barrier, inc=1, device_id=sibling, device_id_type=MESH)
    pl.semaphore_wait(barrier, 10)

    def copy(src, dst, slot, peer):
        return pltpu.make_async_remote_copy(
            src, dst, sends.at[slot], recvs.at[slot], device_id=peer, device_id_type=MESH
        )

    def quarter(owner_x):
        return rows.at[y, owner_x]

    @pl.when(x == 0)
    def _():
        out = [copy(column.at[d], rows.at[y, d], d - 1, at_x(d)) for d in (1, 2, 3)]
        for one in out:
            one.start()
        own = pltpu.make_async_copy(column.at[0], rows.at[y, 0], local)
        own.start()
        own.wait()
        for one in out:
            one.wait_send()

    for d in (1, 2, 3):

        @pl.when(x == d)
        def _(d=d):
            copy(column.at[d], rows.at[y, d], d - 1, at_x(4 - d)).wait_recv()

    first = []
    for d in (1, 2, 3):
        half = rows.at[y, x, 0]
        first.append(copy(half, half, 2 + d, at_x(d)))
        half = rows.at[y, x, 1]
        first.append(copy(half, half, 5 + d, at_y(d)))
    for one in first:
        one.start()
    for one in first:
        one.wait()
    second = []
    for d in (1, 2, 3):
        half = rows.at[y, :, 0]
        second.append(copy(half, half, 8 + d, at_y(d)))
        half = rows.at[:, x, 1]
        second.append(copy(half, half, 11 + d, at_x(d)))
    for one in second:
        one.start()
    for one in second:
        one.wait()

    source = lax.rem(q, ROWS)
    lead = source // 2
    for m in range(8):
        l = 2 * m + q // ROWS
        tile = rows.at[:, l // 6, lax.rem(l, 6) // 3, lax.rem(l, 3)]

        @pl.when(p == source)
        def _(m=m, tile=tile):
            own = pltpu.make_async_copy(tile, cols.at[m], local)
            own.start()
            own.wait()

    @pl.when(p == source)
    def _():
        out = [copy(cols, cols, 14 + d, at_z(d)) for d in (1, 2, 3)]
        out.append(copy(cols, cols, 18, sibling))
        for one in out:
            one.start()
        for one in out:
            one.wait_send()

    for d in (1, 2, 3):

        @pl.when((core == lax.rem(source, 2)) & (lax.rem(lead + d, 4) == z))
        def _(d=d):
            copy(cols, cols, 14 + d, at_z(4 - d)).wait_recv()
            on = copy(cols, cols, 18, sibling)
            on.start()
            on.wait_send()

    @pl.when(core != lax.rem(source, 2))
    def _():
        copy(cols, cols, 18, sibling).wait_recv()


def spread_panels(column):
    return pl.pallas_call(
        spread_kernel,
        out_shape=(
            jax.ShapeDtypeStruct((4, 4, 2, 3, TILE, TILE), BF16),
            jax.ShapeDtypeStruct((8, 4, TILE, TILE), BF16),
        ),
        in_specs=[spec(pltpu.VMEM)],
        out_specs=(spec(pltpu.VMEM), spec(pltpu.VMEM)),
        scratch_shapes=[
            pltpu.SemaphoreType.DMA((19,)),
            pltpu.SemaphoreType.DMA((19,)),
            pltpu.SemaphoreType.DMA,
        ],
        compiler_params=pltpu.CompilerParams(
            collective_id=2, has_side_effects=True, vmem_limit_bytes=VMEM_LIMIT
        ),
        cost_estimate=pl.CostEstimate(flops=0, bytes_accessed=2**23, transcendentals=0),
        name="spread",
    )(column)


def finish_kernel(
    targets,
    where,
    front,
    arrived,
    rows,
    cols,
    lower,
    inverse,
    out,
    factor_cols,
    row_from,
    col_from,
    seen,
):
    l = pl.program_id(0)
    p = where[0]
    q = where[1]

    @pl.when(l == 0)
    def _():
        index_rows(targets, p, row_from, seen)
        index_cols(targets, q, col_from)
        for m in range(8):
            wide = jnp.concatenate([cols[m, f] for f in range(4)], axis=1)
            solved = lax.dot_general(wide, inverse[...], NT, preferred_element_type=F32)
            factor_cols[m * TILE : (m + 1) * TILE, :] = solved.astype(BF16)

        @pl.when(q < 4)
        def _():
            factor_cols[:TILE, :] = jnp.zeros((TILE, 4 * TILE), BF16)

    natural = l * ROWS + p
    wide = jnp.concatenate([rows[f, 0, 0, 0] for f in range(4)], axis=1)
    solved = lax.dot_general(wide, inverse[...], NT, preferred_element_type=F32)
    pivot = jnp.concatenate([lower[jnp.minimum(natural, 3) * 4 + f] for f in range(4)], axis=1)
    solved = jnp.where(natural < 4, pivot, solved)
    panel_of = lax.broadcasted_iota(jnp.int32, (TILE, 4 * TILE), 1) // 256
    live = jnp.where(panel_of < natural // 2, solved, 0.0)
    product = lax.dot_general(
        live.astype(BF16), factor_cols[...], NT, preferred_element_type=F32
    )
    out[...] = front[...].astype(F32) - product
    for c in range(2):
        row = row_from[c * 24 + l]
        for m in range(8):
            col = col_from[c * 8 + m]

            @pl.when((row >= 0) & (col >= 0))
            def _(row=row, col=col, m=m):
                out[:, m * TILE : (m + 1) * TILE] += arrived[row + col].astype(F32)

    for f in range(4):

        @pl.when(q == f)
        def _(f=f):
            out[:, :TILE] = solved[:, f * TILE : (f + 1) * TILE]


def finish(targets, where, front, arrived, rows, cols, lower, inverse):
    return pl.pallas_call(
        finish_kernel,
        out_shape=jax.ShapeDtypeStruct((24 * TILE, 8 * TILE), F32),
        grid=(24,),
        in_specs=[
            spec(pltpu.SMEM),
            spec(pltpu.SMEM),
            pl.BlockSpec((TILE, 8 * TILE), lambda l: (l, 0)),
            spec(pltpu.VMEM),
            pl.BlockSpec(
                (4, 1, 1, 1, TILE, TILE), lambda l: (0, l // 6, l % 6 // 3, l % 3, 0, 0)
            ),
            spec(pltpu.VMEM),
            spec(pltpu.VMEM),
            spec(pltpu.VMEM),
        ],
        out_specs=pl.BlockSpec((TILE, 8 * TILE), lambda l: (l, 0)),
        scratch_shapes=[
            pltpu.VMEM((8 * TILE, 4 * TILE), BF16),
            pltpu.SMEM((48,), jnp.int32),
            pltpu.SMEM((16,), jnp.int32),
            pltpu.SMEM((ROWS,), jnp.int32),
        ],
        compiler_params=pltpu.CompilerParams(vmem_limit_bytes=VMEM_LIMIT),
        cost_estimate=pl.CostEstimate(flops=2**33, bytes_accessed=32 * 2**20, transcendentals=0),
        name="finish",
    )(targets, where, front, arrived, rows, cols, lower, inverse)


def shards(front_block, child_blocks, row_offsets, tile_targets):
    where = jnp.stack([lax.axis_index("row"), lax.axis_index("col")]).astype(jnp.int32)
    offsets = row_offsets.reshape(2, 128, TILE)
    picked, corner_part = place(
        tile_targets, where, offsets, child_blocks, front_block[:TILE, :TILE]
    )
    arrived = lax.all_to_all(
        picked.reshape(DEVICES, 2, TILE, TILE), ("row", "col"), 0, 0, tiled=True
    ).reshape(DEVICES * 2, TILE, TILE)
    corner = sum_corner(corner_part.reshape(DEVICES, 16, TILE))
    lower, inverse = factor(corner.reshape(16, TILE, TILE))
    column = first_column(tile_targets, where, front_block, arrived)
    rows, cols = spread_panels(column.reshape(4, 2, 3, TILE, TILE))
    return finish(tile_targets, where, front_block, arrived, rows, cols, lower, inverse)


def solution(mesh):
    return jax.shard_map(
        shards,
        mesh=mesh,
        in_specs=(P("row", "col"), P(None, "row", "col"), P(), P()),
        out_specs=P("row", "col"),
        check_vma=False,
    )
```

time: 965 us -> 335 us (0.35)
  waiting for transfers between devices: 462 us -> 0.01 us
  Pallas kernels: 0 us -> 315 us
  other arithmetic: 232 us -> 0.59 us
  local copies, waits for them, and re-layouts: 187 us -> 2.94 us
  matrix products: 44.5 us -> 0 us
  between operations: 17.1 us -> 0.03 us
    psum x6 -> x0, waiting for transfers between devices: 404 us -> none  [spread(): return lax.psum(kept, axis)]
    pallas_call x0 -> x6, Pallas kernels: none -> 315 us  [the longest x1 133 us: sum_corner(): pl.pallas_call(corner_kernel, out_shape=jax.ShapeDtypeStruct((DEVICES, 16...]
    another operation x20 -> x1, other arithmetic: 117 us -> 0.59 us  [shards(): jnp.stack([lax.axis_index('row'), lax.axis_index('col')]).astype(jnp.int32)]
    gather x12 -> x0, local copies, waits for them, and re-layouts: 60 us -> none  [the longest x4 32.4 us: shards(): inside = pivot_block[jnp.clip(relative, 0, PANEL - 1)]]
    all_to_all x1, waiting for transfers between devices: 57.9 us -> 0.01 us  [shards(): lax.all_to_all(picked.reshape(DEVICES, 2, TILE, TILE), ('row', 'col'), 0,...]
    scatter-add x1 -> x0, other arithmetic: 53.8 us -> none  [shards(): summed.at[front_rows, :, front_cols, :].add(arrived_tiles, mode='drop')]
    unnamed x60 -> x1, local copies, waits for them, and re-layouts: 43.7 us -> 1.56 us
    dot_general x3 -> x0, matrix products: 31 us -> none  [the longest x2 24.5 us: update_block(): jnp.dot(factor_rows, factor_cols.T, precision=lax.Precision.HIGHEST, pref...]
  transfers between devices with their start and end apart: 7 -> 1, of which waited for: 7 -> 0; matrix products, arithmetic and copies ran while one was open for 5% -> 0% of each run, Pallas kernels for 0% -> 56%
where the time goes in v1:
time: 335 us; the launch traced here: 331 us
  Pallas kernels  315 us (94%)
  starting transfers between devices  11.7 us (3%)
    pallas_call x1, Pallas kernels, sum_corner(): pl.pallas_call(corner_kernel, out_shape=jax.ShapeDtypeStruct((DEVICES, 16...  133 us
    pallas_call x1, Pallas kernels, spread_panels(): pl.pallas_call(spread_kernel, out_shape=(jax.ShapeDtypeStruct((4, 4, 2, 3...  65 us
    pallas_call x1, Pallas kernels, factor(): pl.pallas_call(factor_kernel, out_shape=(jax.ShapeDtypeStruct((16, TILE,...  52.4 us
    pallas_call x1, Pallas kernels, finish(): pl.pallas_call(finish_kernel, out_shape=jax.ShapeDtypeStruct((24 * TILE,...  37.5 us
    pallas_call x1, Pallas kernels, place(): pl.pallas_call(place_kernel, out_shape=(jax.ShapeDtypeStruct((DEVICES * 2...  16.3 us
    all_to_all x1, starting transfers between devices, shards(): lax.all_to_all(picked.reshape(DEVICES, 2, TILE, TILE), ('row', 'col'), 0,...  11.7 us
    pallas_call x1, Pallas kernels, first_column(): pl.pallas_call(column_kernel, out_shape=jax.ShapeDtypeStruct((24, TILE, T...  11.2 us
  transfers between devices with their start and end apart: 1, of which 0 were waited for; matrix products, arithmetic and copies ran while one was open for 0% of the time, Pallas kernels for 56%

profile of v1, /device:TPU:0, one launch (start us, length us, event | category | flops | bytes accessed | tf_op | source)
XLA Modules:
  0.0 330.6 jit_solution(12271020717889587838)
XLA Ops:
  0.0 1.4 slice.3.front
  1.4 1.6 copy.7
  2.9 0.6 pad_add_fusion.where
  3.5 16.3 %place.1 = (bf16[256,128,128]{2,1,0:T(8,128)(2,1)}, f32[16,128,128]{2,1,0:T(8,128)}) custom-call(s32[2,128]{1,0:T(2,128)} %targets.5, s32[2]{0:T(128)} %pad_add_fusion.where, s32[2,128,128]{2,1,0:T(8,128)} %bitcast.16, bf16[2,2048,512]{2,1,0:T(8,128)(2,1)} %child.1, bf16[128,128]{1,0:T(8,128)(2,1)} %slice.3.front), custom_call_target="tpu_custom_call" | custom-call | flops 2147483648 | bytes 14680064 | tf_op jit(solution)/shard_map/place/pallas_call | solution.py:79
  19.9 11.7 %all-to-all-start = ((bf16[128,2,128,128]{3,2,1,0:T(8,128)(2,1)}), bf16[128,2,128,128]{3,2,1,0:T(8,128)(2,1)}, u32[]{:S(2)}, u32[]{:S(2)}) async-start(bf16[128,2,128,128]{3,2,1,0:T(8,128)(2,1)} %bitcast.11), calls=%async_computation | async-start | bytes 16777216 | tf_op jit(solution)/shard_map/all_to_all | solution.py:575
  31.5 133.0 %corner.1 = f32[128,16,128]{2,1,0:T(8,128)} custom-call(f32[128,16,128]{2,1,0:T(8,128)} %bitcast.13), custom_call_target="tpu_custom_call" | custom-call | flops 262144 | bytes 4194304 | tf_op jit(solution)/shard_map/corner/pallas_call | solution.py:153
  164.5 52.4 %factor.1 = (f32[16,128,128]{2,1,0:T(8,128)}, bf16[512,512]{1,0:T(8,128)(2,1)}) custom-call(f32[16,128,128]{2,1,0:T(8,128)} %bitcast.14), custom_call_target="tpu_custom_call" | custom-call | flops 1073741824 | bytes 4194304 | tf_op jit(solution)/shard_map/factor/pallas_call | solution.py:250
  216.9 0.0 all-to-all-done
  216.9 11.2 %column.1 = bf16[24,128,128]{2,1,0:T(8,128)(2,1)} custom-call(s32[2,128]{1,0:T(2,128)} %targets.5, s32[2]{0:T(128)} %pad_add_fusion.where, bf16[3072,1024]{1,0:T(8,128)(2,1)} %front.3, bf16[256,128,128]{2,1,0:T(8,128)(2,1)} %bitcast.3.arrived), custom_call_target="tpu_custom_call" | custom-call | flops 1048576 | bytes 8388608 | tf_op jit(solution)/shard_map/column/pallas_call | solution.py:331
  228.1 65.0 %spread.1 = (bf16[4,4,2,3,128,128]{5,4,3,2,1,0:T(8,128)(2,1)}, bf16[8,4,128,128]{3,2,1,0:T(8,128)(2,1)}) custom-call(bf16[4,2,3,128,128]{4,3,2,1,0:T(8,128)(2,1)} %bitcast.12), custom_call_target="tpu_custom_call" | custom-call | bytes 8388608 | tf_op jit(solution)/shard_map/spread/pallas_call | solution.py:459
  293.1 37.5 %finish.1 = f32[3072,1024]{1,0:T(8,128)} custom-call(s32[2,128]{1,0:T(2,128)} %targets.5, s32[2]{0:T(128)} %pad_add_fusion.where, bf16[3072,1024]{1,0:T(8,128)(2,1)} %front.3, bf16[256,128,128]{2,1,0:T(8,128)(2,1)} %bitcast.3.arrived, bf16[4,4,2,3,128,128]{5,4,3,2,1,0:T(8,128)(2,1)} %get-tuple-element.12.rows, ...), custom_call_target="tpu_custom_call" | custom-call | flops 8589934592 | bytes 33554432 | tf_op jit(solution)/shard_map/finish/pallas_call | solution.py:540
Async XLA Ops:
  19.9 197.0 %all-to-all-start = ((bf16[128,2,128,128]{3,2,1,0:T(8,128)(2,1)}), bf16[128,2,128,128]{3,2,1,0:T(8,128)(2,1)}, u32[]{:S(2)}, u32[]{:S(2)}) async-start(bf16[128,2,128,128]{3,2,1,0:T(8,128)(2,1)} %bitcast.11), calls=%async_computation | async-start | bytes 16777216 | tf_op jit(solution)/shard_map/all_to_all | solution.py:575
